TPU v7x, 512 devices: a whole 4x8x8 slice. The times are simulated.
512 devices in a mesh: section: 64 (over y_hi, z, core), dp: 8 (over y_lo, x).
Axes of the slice: x: 4, y: 8 (y_hi: 4, y_lo: 2; y = y_hi * 2 + y_lo), z: 8, core: 2. Of those that a mesh axis runs over, the one named last changes fastest.
Arguments:
- qkv_weight: bfloat16 [2, 64, 512, 1536], P(None, 'section', 'dp'), may hold values from -0.25 to 0.25
- out_weight: bfloat16 [2, 64, 512, 512], P(None, 'section', 'dp'), may hold values from -0.25 to 0.25
- activations: bfloat16 [2, 64, 8, 128, 512], P(None, 'section', 'dp'), may hold values from -60 to 60
- cotangents: bfloat16 [2, 64, 8, 128, 512], P(None, 'section', 'dp'), may hold values from -6 to 6
- mirrored_stash: bfloat16 [2, 2, 64, 8, 128, 512], P(None, None, 'section', 'dp'), may hold values from -60 to 60
- arrivals: bfloat16 [2, 8, 128, 512], P(None, 'dp'), may hold values from -60 to 60
- head_grads: bfloat16 [2, 8, 128, 512], P(None, 'dp'), may hold values from -6 to 6
Outputs:
- qkv_grad: float32 [2, 64, 512, 1536], P(None, 'section', 'dp')
- out_grad: float32 [2, 64, 512, 512], P(None, 'section', 'dp')
- new_activations: bfloat16 [2, 64, 8, 128, 512], P(None, 'section', 'dp')
- new_cotangents: bfloat16 [2, 64, 8, 128, 512], P(None, 'section', 'dp')
Inputs may be any that keep to these rules, and one draw needn't show every extreme that they name: `qkv_weight`: every attention score q k^T / sqrt(64) that the layers form from the given inputs lies within -80 to 80.
All inputs are finite; a program needn't handle non-finite values.
Results may differ from a plain program's by a relative error of at most 0.025.
Values may be sent and summed in bfloat16 or wider, within the bound.
A program may use at most 64 MiB of HBM per device.

v0:
```python
import jax
import jax.numpy as jnp
from jax import lax
from jax.sharding import PartitionSpec as P

HEADS = 8
HEAD = 64


def passed_along(shard, axis, by):
    size = lax.axis_size(axis)
    return lax.ppermute(shard, axis, [(i, (i + by) % size) for i in range(size)])


def from_partner(shard, axis, distance):
    return lax.ppermute(shard, axis, [(i, i ^ 1 << distance) for i in range(lax.axis_size(axis))])


def attend(inputs, qkv_part, out_part):
    row_count = inputs.shape[0]
    feat_width = inputs.shape[1]
    floats = inputs.astype(jnp.float32)
    factor = lax.rsqrt(jnp.mean(floats * floats, axis=-1, keepdims=True) + 1e-05)
    normed = (floats * factor).astype(jnp.bfloat16)
    packed = jnp.dot(normed, qkv_part, preferred_element_type=jnp.float32).astype(jnp.bfloat16)
    queries = packed[:, :feat_width].reshape(row_count, HEADS, HEAD).astype(jnp.float32)
    key_rows = (
        packed[:, feat_width : 2 * feat_width].reshape(row_count, HEADS, HEAD).astype(jnp.float32)
    )
    values = packed[:, 2 * feat_width :].reshape(row_count, HEADS, HEAD).astype(jnp.float32)
    scores = jnp.einsum("qhd,khd->hqk", queries, key_rows) * HEAD ** (-0.5)
    query_pos = lax.broadcasted_iota(jnp.int32, (row_count, row_count), 0)
    key_pos = lax.broadcasted_iota(jnp.int32, (row_count, row_count), 1)
    causal = (key_pos <= query_pos)[None]
    raised = jnp.where(causal, jnp.exp(scores), jnp.zeros_like(scores))
    soft_weights = (raised / jnp.sum(raised, axis=-1, keepdims=True)).astype(jnp.bfloat16)
    context = jnp.einsum("hqk,khd->qhd", soft_weights.astype(jnp.float32), values)
    context = context.astype(jnp.bfloat16).reshape(row_count, feat_width)
    mixed = jnp.dot(context, out_part, preferred_element_type=jnp.float32)
    return (floats + mixed).astype(jnp.bfloat16)


def full_pull(inputs, grads_in, qkv_part, out_part):
    unused, pull = jax.vjp(attend, inputs, qkv_part, out_part)
    return pull(grads_in)


def shards(qkv_weight, out_weight, activations, cotangents, mirrored_stash, arrivals, head_grads):
    qkv_full, out_full = (
        lax.all_gather(qkv_weight, "dp", axis=2, tiled=True),
        lax.all_gather(out_weight, "dp", axis=2, tiled=True),
    )
    qkv_full = qkv_full[:, 0]
    out_full = out_full[:, 0]
    forward_state = activations[:, 0]
    back_state = cotangents[:, 0]
    section_count = lax.axis_size("section")
    position = lax.axis_index("section")
    top_bit = section_count.bit_length() - 2
    tick_count = mirrored_stash.shape[0]
    qkv_sums = [
        jnp.zeros(qkv_full.shape[1:], jnp.float32),
        jnp.zeros(qkv_full.shape[1:], jnp.float32),
    ]
    out_sums = [
        jnp.zeros(out_full.shape[1:], jnp.float32),
        jnp.zeros(out_full.shape[1:], jnp.float32),
    ]
    for step_index in range(tick_count):
        layer_out = jnp.stack(
            [
                attend(forward_state[virtual, 0], qkv_full[virtual], out_full[virtual])[None]
                for virtual in range(2)
            ]
        )
        arrived_fwd = passed_along(layer_out, "section", 1)
        at_first = position == 0
        forward_state = jnp.where(
            at_first, jnp.stack([arrivals[step_index], arrived_fwd[0]]), arrived_fwd
        )
        current_stash = from_partner(mirrored_stash[step_index, :, 0], "section", top_bit)
        input_cots = [None, None]
        for virtual in (1, 0):
            pulled = full_pull(
                current_stash[virtual, 0],
                back_state[virtual, 0],
                qkv_full[virtual],
                out_full[virtual],
            )
            input_cots[virtual] = pulled[0][None]
            qkv_sums[virtual] = qkv_sums[virtual] + pulled[1].astype(jnp.float32)
            out_sums[virtual] = out_sums[virtual] + pulled[2].astype(jnp.float32)
        stacked_cots = jnp.stack(input_cots)
        arrived_back = passed_along(stacked_cots, "section", -1)
        at_last = position == section_count - 1
        back_state = jnp.where(
            at_last, jnp.stack([arrived_back[1], head_grads[step_index]]), arrived_back
        )
    qkv_first, qkv_second, out_first, out_second = (
        lax.psum_scatter(
            qkv_sums[0].astype(jnp.bfloat16), "dp", scatter_dimension=0, tiled=True
        ).astype(jnp.float32),
        lax.psum_scatter(
            qkv_sums[1].astype(jnp.bfloat16), "dp", scatter_dimension=0, tiled=True
        ).astype(jnp.float32),
        lax.psum_scatter(
            out_sums[0].astype(jnp.bfloat16), "dp", scatter_dimension=0, tiled=True
        ).astype(jnp.float32),
        lax.psum_scatter(
            out_sums[1].astype(jnp.bfloat16), "dp", scatter_dimension=0, tiled=True
        ).astype(jnp.float32),
    )
    qkv_grad = jnp.stack([qkv_first, qkv_second])
    out_grad = jnp.stack([out_first, out_second])
    return (qkv_grad[:, None], out_grad[:, None], forward_state[:, None], back_state[:, None])


def solution(mesh):
    return jax.shard_map(
        shards,
        mesh=mesh,
        in_specs=(
            P(None, "section", "dp", None),
            P(None, "section", "dp", None),
            P(None, "section", "dp", None, None),
            P(None, "section", "dp", None, None),
            P(None, None, "section", "dp", None, None),
            P(None, "dp", None, None),
            P(None, "dp", None, None),
        ),
        out_specs=(
            P(None, "section", "dp", None),
            P(None, "section", "dp", None),
            P(None, "section", "dp", None, None),
            P(None, "section", "dp", None, None),
        ),
        check_vma=False,
    )
```

profile of v0, /device:TPU:16, one launch (start us, length us, event | category | flops | bytes accessed | tf_op | source)
XLA Modules:
  0.0 352.7 jit_solution(6664824194356118152)
XLA Ops:
  8.7 1.1 slice_bitcast_fusion.25
  9.8 5.9 %collective-permute-start = (bf16[2,1,128,512]{3,2,1,0:T(8,128)(2,1)S(1)}, bf16[2,1,128,512]{3,2,1,0:T(8,128)(2,1)S(1)}, u32[]{:S(2)}, u32[]{:S(2)}) collective-permute-start(bf16[2,1,128,512]{3,2,1,0:T(8,128)(2,1)S(1)} %get-tuple-element.37), channel_id=1, source_target_pairs={{0,256},{8,264},{16,272},{24,280},{32,288},{40,296},{48,304},{56,3... | collective-permute-start | bytes 786440 | tf_op jit(solution)/shard_map/ppermute | solution.py:16
  15.7 3.8 %collective-permute-start.1 = (bf16[2,1,128,512]{3,2,1,0:T(8,128)(2,1)S(1)}, bf16[2,1,128,512]{3,2,1,0:T(8,128)(2,1)S(1)}, u32[]{:S(2)}, u32[]{:S(2)}) collective-permute-start(bf16[2,1,128,512]{3,2,1,0:T(8,128)(2,1)S(1)} %get-tuple-element.38), channel_id=1, source_target_pairs={{0,256},{8,264},{16,272},{24,280},{32,288},{40,296},{48,304},{56,3... | collective-permute-start | bytes 786440 | tf_op jit(solution)/shard_map/ppermute | solution.py:16
  19.7 0.7 fusion.172
  20.5 7.9 %collective-permute-done = bf16[2,1,128,512]{3,2,1,0:T(8,128)(2,1)S(1)} collective-permute-done((bf16[2,1,128,512]{3,2,1,0:T(8,128)(2,1)S(1)}, bf16[2,1,128,512]{3,2,1,0:T(8,128)(2,1)S(1)}, u32[]{:S(2)}, u32[]{:S(2)}) %collective-permute-start) | collective-permute-done | bytes 262176 | tf_op jit(solution)/shard_map/ppermute | solution.py:16
  28.4 9.6 %collective-permute-done.1 = bf16[2,1,128,512]{3,2,1,0:T(8,128)(2,1)S(1)} collective-permute-done((bf16[2,1,128,512]{3,2,1,0:T(8,128)(2,1)S(1)}, bf16[2,1,128,512]{3,2,1,0:T(8,128)(2,1)S(1)}, u32[]{:S(2)}, u32[]{:S(2)}) %collective-permute-start.1) | collective-permute-done | bytes 262176 | tf_op jit(solution)/shard_map/ppermute | solution.py:16
  38.7 22.3 %all-gather.3.cloned.1.call-done = bf16[2,1,512,512]{3,2,1,0:T(8,128)(2,1)} async-done(((bf16[2,1,64,512]{3,2,1,0:T(8,128)(2,1)}), bf16[2,1,512,512]{3,2,1,0:T(8,128)(2,1)}) %all-gather.3.cloned.1.call-update) | async-done | bytes 1048592 | tf_op jit(solution)/shard_map/all_gather | solution.py:51
  61.0 1.3 convolution_convert_fusion.39
  62.5 1.4 convolution_convert_fusion.43
  64.0 48.8 %all-gather.5.cloned.1.call-done = bf16[2,1,512,1536]{3,2,1,0:T(8,128)(2,1)} async-done(((bf16[2,1,64,1536]{3,2,1,0:T(8,128)(2,1)}), bf16[2,1,512,1536]{3,2,1,0:T(8,128)(2,1)}) %all-gather.5.cloned.1.call-update) | async-done | bytes 3145744 | tf_op jit(solution)/shard_map/all_gather | solution.py:50
  112.8 1.8 convolution_convert_fusion.11
  116.3 0.9 convolution_convert_fusion.27
  118.7 2.8 fusion.63
  123.2 1.7 select_reduce_fusion.1
  125.9 0.9 convolution_convert_fusion.25
  128.3 0.8 copy.115
  129.1 1.8 convolution_convert_fusion.7
  131.2 0.8 copy.111
  132.0 1.8 convolution_convert_fusion.8
  134.8 2.1 fusion.58
  137.2 0.7 pad_maximum_fusion
  137.9 2.6 collective-permute-start.2
  140.9 0.9 convolution_convert_fusion.22
  142.1 1.9 convolution_convert_fusion.23
  144.0 1.1 fusion.16
  145.1 1.8 fusion.34
  146.9 0.9 fusion.35
  147.8 0.8 copy.104
  148.6 0.8 copy.97
  149.3 1.2 fusion.3
  150.5 0.9 maximum_select_fusion
  151.8 0.8 copy.93
  152.8 0.8 copy.100
  153.6 3.1 multiply_reduce_fusion.1
  156.7 1.7 divide_convert_fusion.4
  158.4 0.7 copy-done.3
  159.3 1.1 fusion.2
  160.5 1.8 pad_maximum_fusion.1
  162.3 1.9 collective-permute-start.3
  164.2 1.2 fusion.7
  166.7 1.6 convolution_convert_fusion.28
  168.2 1.1 fusion.6
  169.6 1.2 convolution_convert_fusion.30
  170.8 1.3 convolution_convert_fusion.29
  173.5 1.8 add_convert_fusion
  175.5 0.9 copy-done.25
  177.2 1.9 convolution_convert_fusion.4
  181.2 1.5 convolution_convert_fusion.32
  184.5 1.9 add_convert_fusion.1
  187.0 1.9 convolution_convert_fusion.5
  189.3 0.8 copy.119
  190.8 1.2 convolution_convert_fusion.21
  192.3 3.2 collective-permute-start.4
  195.6 2.1 fusion.28
  197.7 0.7 fusion.67
  198.8 5.7 %collective-permute-start.5 = (bf16[2,1,128,512]{3,2,1,0:T(8,128)(2,1)S(1)}, bf16[2,1,128,512]{3,2,1,0:T(8,128)(2,1)S(1)}, u32[]{:S(2)}, u32[]{:S(2)}) collective-permute-start(bf16[2,1,128,512]{3,2,1,0:T(8,128)(2,1)S(1)} %pad_maximum_fusion.3), channel_id=1, source_target_pairs={{0,504},{8,0},{16,8},{24,16},{32,24},{40,32},{48,40},{56,48},{64,5... | collective-permute-start | bytes 786440 | tf_op jit(solution)/shard_map/ppermute | solution.py:12
  204.5 6.7 %collective-permute-done.5 = bf16[2,1,128,512]{3,2,1,0:T(8,128)(2,1)S(1)} collective-permute-done((bf16[2,1,128,512]{3,2,1,0:T(8,128)(2,1)S(1)}, bf16[2,1,128,512]{3,2,1,0:T(8,128)(2,1)S(1)}, u32[]{:S(2)}, u32[]{:S(2)}) %collective-permute-start.5) | collective-permute-done | bytes 262176 | tf_op jit(solution)/shard_map/ppermute | solution.py:12
  211.2 0.7 fusion.85
  211.9 0.7 fusion.86
  212.7 35.6 %reduce-scatter.9.cloned.1.call-done = bf16[64,512]{1,0:T(8,128)(2,1)} async-done(((bf16[512,512]{1,0:T(8,128)(2,1)}), bf16[64,512]{1,0:T(8,128)(2,1)}) %reduce-scatter.9.cloned.1.call-update) | async-done | bytes 65552 | tf_op jit(solution)/shard_map/reduce_scatter | solution.py:106
  248.2 1.6 fusion.115
  249.8 46.3 %reduce-scatter.7.cloned.1.call-done = bf16[64,1536]{1,0:T(8,128)(2,1)} async-done(((bf16[512,1536]{1,0:T(8,128)(2,1)}), bf16[64,1536]{1,0:T(8,128)(2,1)}) %reduce-scatter.7.cloned.1.call-update) | async-done | bytes 196624 | tf_op jit(solution)/shard_map/reduce_scatter | solution.py:103
  296.1 47.8 %reduce-scatter.5.cloned.1.call-done = bf16[64,1536]{1,0:T(8,128)(2,1)} async-done(((bf16[512,1536]{1,0:T(8,128)(2,1)}), bf16[64,1536]{1,0:T(8,128)(2,1)}) %reduce-scatter.5.cloned.1.call-update) | async-done | bytes 196624 | tf_op jit(solution)/shard_map/reduce_scatter | solution.py:100
  343.9 2.0 fusion.36
  (258 shorter events, 22.5 us)
Async XLA Ops:
  7.2 12.4 %copy-start.2 = (bf16[2,1,1,128,512]{4,3,2,1,0:T(8,128)(2,1)S(1)}, bf16[2,1,1,128,512]{4,3,2,1,0:T(8,128)(2,1)}, u32[]{:S(2)}) copy-start(bf16[2,1,1,128,512]{4,3,2,1,0:T(8,128)(2,1)} %param.9) | copy-start | bytes 786436
  7.2 12.5 %copy-start.24 = (bf16[2,1,128,512]{3,2,1,0:T(8,128)(2,1)S(1)}, bf16[2,1,128,512]{3,2,1,0:T(8,128)(2,1)}, u32[]{:S(2)}) copy-start(bf16[2,1,128,512]{3,2,1,0:T(8,128)(2,1)} %param.13) | copy-start | bytes 786436
  7.2 53.9 %copy-start.1 = (bf16[2,1,1,128,512]{4,3,2,1,0:T(8,128)(2,1)S(1)}, bf16[2,1,1,128,512]{4,3,2,1,0:T(8,128)(2,1)}, u32[]{:S(2)}) copy-start(bf16[2,1,1,128,512]{4,3,2,1,0:T(8,128)(2,1)} %param.10) | copy-start | bytes 786436
  7.2 53.8 %all-gather.3.cloned.1.call-start = ((), (), s32[]{:S(2)}) async-start(), calls=%async_computation.4 | async-start | bytes 1179648 | tf_op jit(solution)/shard_map/all_gather | solution.py:51
  7.9 104.9 %all-gather.5.cloned.1.call-start = ((), (), s32[]{:S(2)}) async-start(), calls=%async_computation.5 | async-start | bytes 3538944 | tf_op jit(solution)/shard_map/all_gather | solution.py:50
  8.7 204.0 %reduce-scatter.11.cloned.1.call-start = ((), (), s32[]{:S(2)}) async-start(), calls=%async_computation.9 | async-start | bytes 589824 | tf_op jit(solution)/shard_map/reduce_scatter | solution.py:109
  9.8 18.5 %collective-permute-start = (bf16[2,1,128,512]{3,2,1,0:T(8,128)(2,1)S(1)}, bf16[2,1,128,512]{3,2,1,0:T(8,128)(2,1)S(1)}, u32[]{:S(2)}, u32[]{:S(2)}) collective-permute-start(bf16[2,1,128,512]{3,2,1,0:T(8,128)(2,1)S(1)} %get-tuple-element.37), channel_id=1, source_target_pairs={{0,256},{8,264},{16,272},{24,280},{32,288},{40,296},{48,304},{56,3... | collective-permute-start | bytes 786440 | tf_op jit(solution)/shard_map/ppermute | solution.py:16
  15.7 22.3 %collective-permute-start.1 = (bf16[2,1,128,512]{3,2,1,0:T(8,128)(2,1)S(1)}, bf16[2,1,128,512]{3,2,1,0:T(8,128)(2,1)S(1)}, u32[]{:S(2)}, u32[]{:S(2)}) collective-permute-start(bf16[2,1,128,512]{3,2,1,0:T(8,128)(2,1)S(1)} %get-tuple-element.38), channel_id=1, source_target_pairs={{0,256},{8,264},{16,272},{24,280},{32,288},{40,296},{48,304},{56,3... | collective-permute-start | bytes 786440 | tf_op jit(solution)/shard_map/ppermute | solution.py:16
  28.4 9.8 %copy-start.65 = (f32[128]{0:T(128)}, f32[128]{0:T(128)S(1)}, u32[]{:S(2)}) copy-start(f32[128]{0:T(128)S(1)} %fusion.61) | copy-start | bytes 1540
  38.2 74.6 %copy-start.59 = (f32[128]{0:T(128)}, f32[128]{0:T(128)S(1)}, u32[]{:S(2)}) copy-start(f32[128]{0:T(128)S(1)} %fusion.148) | copy-start | bytes 1540
  38.2 79.2 %copy-start.49 = (f32[128]{0:T(128)}, f32[128]{0:T(128)S(1)}, u32[]{:S(2)}) copy-start(f32[128]{0:T(128)S(1)} %fusion.149) | copy-start | bytes 1540
  38.7 93.2 %copy-start.52 = (f32[128]{0:T(128)}, f32[128]{0:T(128)S(1)}, u32[]{:S(2)}) copy-start(f32[128]{0:T(128)S(1)} %fusion.151) | copy-start | bytes 1540
  115.9 2.8 copy-start.26
  115.9 2.0 copy-start.67
  116.3 2.5 copy-start.28
  118.6 4.7 %copy-start.21 = (bf16[128,512]{0,1:T(8,128)(2,1)}, bf16[128,512]{0,1:T(8,128)(2,1)S(1)}, u32[]{:S(2)}) copy-start(bf16[128,512]{0,1:T(8,128)(2,1)S(1)} %copy.95) | copy-start | bytes 393220
  118.7 4.5 %copy-start.22 = (bf16[128,512]{0,1:T(8,128)(2,1)}, bf16[128,512]{0,1:T(8,128)(2,1)S(1)}, u32[]{:S(2)}) copy-start(bf16[128,512]{0,1:T(8,128)(2,1)S(1)} %copy.94) | copy-start | bytes 393220
  118.7 3.3 copy-start.68
  125.6 9.2 %copy-start.30 = (bf16[8,128,64]{1,2,0:T(8,128)(2,1)}, bf16[8,128,64]{1,2,0:T(8,128)(2,1)S(1)}, u32[]{:S(2)}) copy-start(bf16[8,128,64]{1,2,0:T(8,128)(2,1)S(1)} %convolution_convert_fusion.36) | copy-start | bytes 393220
  125.6 2.0 copy-start.69
  125.9 8.9 %copy-start.32 = (bf16[8,128,64]{1,2,0:T(8,128)(2,1)}, bf16[8,128,64]{1,2,0:T(8,128)(2,1)S(1)}, u32[]{:S(2)}) copy-start(bf16[8,128,64]{1,2,0:T(8,128)(2,1)S(1)} %convolution_convert_fusion.37) | copy-start | bytes 393220
  127.0 7.8 %copy-start.7 = (bf16[8,64,128]{2,1,0:T(8,128)(2,1)}, bf16[8,64,128]{2,1,0:T(8,128)(2,1)S(1)}, u32[]{:S(2)}) copy-start(bf16[8,64,128]{2,1,0:T(8,128)(2,1)S(1)} %convolution_convert_fusion.38) | copy-start | bytes 393220
  132.0 2.2 copy-start.66
  132.0 2.2 copy-start.73
  132.0 2.2 copy-start.44
  134.0 10.0 %copy-start.12 = (bf16[128,512]{0,1:T(8,128)(2,1)}, bf16[128,512]{0,1:T(8,128)(2,1)S(1)}, u32[]{:S(2)}) copy-start(bf16[128,512]{0,1:T(8,128)(2,1)S(1)} %copy.102) | copy-start | bytes 393220
  134.1 9.9 %copy-start.9 = (bf16[128,512]{0,1:T(8,128)(2,1)}, bf16[128,512]{0,1:T(8,128)(2,1)S(1)}, u32[]{:S(2)}) copy-start(bf16[128,512]{0,1:T(8,128)(2,1)S(1)} %copy.101) | copy-start | bytes 393220
  134.8 2.2 copy-start.72
  134.8 2.2 copy-start.60
  134.8 2.2 copy-start.63
  136.9 4.0 %copy-start.43 = (bf16[128,512]{0,1:T(8,128)(2,1)S(1)}, bf16[128,512]{0,1:T(8,128)(2,1)}, u32[]{:S(2)}) copy-start(bf16[128,512]{0,1:T(8,128)(2,1)} %copy.115) | copy-start | bytes 393220
  137.9 12.6 %collective-permute-start.2 = (bf16[2,1,128,512]{3,2,1,0:T(8,128)(2,1)}, bf16[2,1,128,512]{3,2,1,0:T(8,128)(2,1)S(1)}, u32[]{:S(2)}, u32[]{:S(2)}) collective-permute-start(bf16[2,1,128,512]{3,2,1,0:T(8,128)(2,1)} %pad_maximum_fusion), channel_id=1, source_target_pairs={{0,504},{8,0},{16,8},{24,16},{32,24},{40,32},{48,40},{56,48},{64,5... | collective-permute-start | bytes 786440 | tf_op jit(solution)/shard_map/ppermute | solution.py:12
  142.1 3.0 copy-start
  144.0 2.9 copy-start.42
  153.6 3.1 copy-start.5
  153.6 3.1 copy-start.14
  153.6 3.1 copy-start.17
  156.7 2.6 copy-start.47
  160.4 5.7 %copy-start.15 = (bf16[128,512]{0,1:T(8,128)(2,1)S(1)}, bf16[128,512]{0,1:T(8,128)(2,1)}, u32[]{:S(2)}) copy-start(bf16[128,512]{0,1:T(8,128)(2,1)} %copy.97) | copy-start | bytes 393220
  160.4 6.3 %copy-start.6 = (f32[8,128,128]{1,2,0:T(8,128)S(1)}, f32[8,128,128]{1,2,0:T(8,128)}, u32[]{:S(2)}) copy-start(f32[8,128,128]{1,2,0:T(8,128)} %fusion.16) | copy-start | bytes 1572868
  160.4 6.3 %copy-start.13 = (bf16[128,512]{0,1:T(8,128)(2,1)S(1)}, bf16[128,512]{0,1:T(8,128)(2,1)}, u32[]{:S(2)}) copy-start(bf16[128,512]{0,1:T(8,128)(2,1)} %copy-done.12) | copy-start | bytes 393220
  160.4 87.8 %reduce-scatter.9.cloned.1.call-start = ((), (), s32[]{:S(2)}) async-start(), calls=%async_computation.8 | async-start | bytes 589824 | tf_op jit(solution)/shard_map/reduce_scatter | solution.py:106
  160.5 6.2 %copy-start.76 = (f32[8,128,128]{1,2,0:T(8,128)S(1)}, f32[8,128,128]{1,2,0:T(8,128)}, u32[]{:S(2)}) copy-start(f32[8,128,128]{1,2,0:T(8,128)} %get-tuple-element.76) | copy-start | bytes 1572868
  162.3 14.7 %collective-permute-start.3 = (bf16[2,1,128,512]{3,2,1,0:T(8,128)(2,1)}, bf16[2,1,128,512]{3,2,1,0:T(8,128)(2,1)S(1)}, u32[]{:S(2)}, u32[]{:S(2)}) collective-permute-start(bf16[2,1,128,512]{3,2,1,0:T(8,128)(2,1)} %pad_maximum_fusion.1), channel_id=1, source_target_pairs={{0,8},{8,16},{16,24},{24,32},{32,40},{40,48},{48,56},{56,64},{64,7... | collective-permute-start | bytes 786440 | tf_op jit(solution)/shard_map/ppermute | solution.py:12
  168.2 2.6 copy-start.10
  169.3 126.8 %reduce-scatter.7.cloned.1.call-start = ((), (), s32[]{:S(2)}) async-start(), calls=%async_computation.7 | async-start | bytes 1769472 | tf_op jit(solution)/shard_map/reduce_scatter | solution.py:103
  169.6 3.3 copy-start.34
  169.6 3.2 copy-start.53
  175.4 168.5 %reduce-scatter.5.cloned.1.call-start = ((), (), s32[]{:S(2)}) async-start(), calls=%async_computation.6 | async-start | bytes 1769472 | tf_op jit(solution)/shard_map/reduce_scatter | solution.py:100
  177.2 2.8 copy-start.46
  177.2 3.4 copy-start.11
  180.8 1.9 copy-start.18
  180.9 1.9 copy-start.23
  180.9 1.9 copy-start.45
  187.0 1.9 copy-start.16
  190.8 4.7 %copy-start.35 = (bf16[8,128,64]{1,2,0:T(8,128)(2,1)S(1)}, bf16[8,128,64]{1,2,0:T(8,128)(2,1)}, u32[]{:S(2)}) copy-start(bf16[8,128,64]{1,2,0:T(8,128)(2,1)} %convolution_convert_fusion.28) | copy-start | bytes 393220
  190.8 4.7 %copy-start.37 = (bf16[8,128,64]{1,2,0:T(8,128)(2,1)S(1)}, bf16[8,128,64]{1,2,0:T(8,128)(2,1)}, u32[]{:S(2)}) copy-start(bf16[8,128,64]{1,2,0:T(8,128)(2,1)} %copy-done.36) | copy-start | bytes 393220
  192.3 5.4 %copy-start.70 = (bf16[2,1,512,1536]{3,2,1,0:T(8,128)(2,1)S(1)}, bf16[2,1,512,1536]{3,2,1,0:T(8,128)(2,1)}, u32[]{:S(2)}) copy-start(bf16[2,1,512,1536]{3,2,1,0:T(8,128)(2,1)} %all-gather.5.cloned.1.call-done) | copy-start | bytes 9437188
  192.3 5.3 %copy-start.39 = (bf16[8,128,64]{1,2,0:T(8,128)(2,1)S(1)}, bf16[8,128,64]{1,2,0:T(8,128)(2,1)}, u32[]{:S(2)}) copy-start(bf16[8,128,64]{1,2,0:T(8,128)(2,1)} %copy-done.38) | copy-start | bytes 393220
  192.3 5.3 %copy-start.41 = (bf16[8,128,64]{1,2,0:T(8,128)(2,1)S(1)}, bf16[8,128,64]{1,2,0:T(8,128)(2,1)}, u32[]{:S(2)}) copy-start(bf16[8,128,64]{1,2,0:T(8,128)(2,1)} %copy-done.40) | copy-start | bytes 393220
  192.3 12.1 %collective-permute-start.4 = (bf16[2,1,128,512]{3,2,1,0:T(8,128)(2,1)S(1)}, bf16[2,1,128,512]{3,2,1,0:T(8,128)(2,1)S(1)}, u32[]{:S(2)}, u32[]{:S(2)}) collective-permute-start(bf16[2,1,128,512]{3,2,1,0:T(8,128)(2,1)S(1)} %pad_maximum_fusion.2), channel_id=1, source_target_pairs={{0,8},{8,16},{16,24},{24,32},{32,40},{40,48},{48,56},{56,64},{64,7... | collective-permute-start | bytes 786440 | tf_op jit(solution)/shard_map/ppermute | solution.py:12
  198.4 12.7 %copy-start.20 = (bf16[1,1,128,512]{3,2,1,0:T(8,128)(2,1)S(1)}, bf16[1,1,128,512]{3,2,1,0:T(8,128)(2,1)}, u32[]{:S(2)}) copy-start(bf16[1,1,128,512]{3,2,1,0:T(8,128)(2,1)} %get-tuple-element.65) | copy-start | bytes 393220
  198.5 13.4 %copy-start.19 = (bf16[1,1,128,512]{3,2,1,0:T(8,128)(2,1)S(1)}, bf16[1,1,128,512]{3,2,1,0:T(8,128)(2,1)}, u32[]{:S(2)}) copy-start(bf16[1,1,128,512]{3,2,1,0:T(8,128)(2,1)} %get-tuple-element.63) | copy-start | bytes 393220
  198.8 12.4 %collective-permute-start.5 = (bf16[2,1,128,512]{3,2,1,0:T(8,128)(2,1)S(1)}, bf16[2,1,128,512]{3,2,1,0:T(8,128)(2,1)S(1)}, u32[]{:S(2)}, u32[]{:S(2)}) collective-permute-start(bf16[2,1,128,512]{3,2,1,0:T(8,128)(2,1)S(1)} %pad_maximum_fusion.3), channel_id=1, source_target_pairs={{0,504},{8,0},{16,8},{24,16},{32,24},{40,32},{48,40},{56,48},{64,5... | collective-permute-start | bytes 786440 | tf_op jit(solution)/shard_map/ppermute | solution.py:12
  (25 other events, 24.9 us)
Sparse Core Ops, SparseCore 0:
  10.1 50.8 all-gather.2
  63.1 49.6 all-gather.4
  160.5 42.2 reduce-scatter.10
  206.2 41.9 reduce-scatter.8
  250.9 45.1 reduce-scatter.6
  298.8 45.0 reduce-scatter.4
where the time goes:
time: 354 us; the launch traced here: 353 us
  waiting for transfers between devices  226 us (64%)
  matrix products  58.3 us (16%)
  starting transfers between devices  23.6 us (7%)
  local copies, waits for them, and re-layouts  17.5 us (5%)
  between operations  15.6 us (4%)
  other arithmetic  11.4 us (3%)
    all_gather x1, waiting for transfers between devices, shards(): lax.all_gather(qkv_weight, 'dp', axis=2, tiled=True)  48.8 us
    reduce_scatter x1, waiting for transfers between devices, shards(): lax.psum_scatter(qkv_sums[0].astype(jnp.bfloat16), 'dp', scatter_dimensio...  47.8 us
    reduce_scatter x1, waiting for transfers between devices, shards(): lax.psum_scatter(qkv_sums[1].astype(jnp.bfloat16), 'dp', scatter_dimensio...  46.3 us
    reduce_scatter x1, waiting for transfers between devices, shards(): lax.psum_scatter(out_sums[0].astype(jnp.bfloat16), 'dp', scatter_dimensio...  35.6 us
    dot_general x16, matrix products, attend(): jnp.dot(normed, qkv_part, preferred_element_type=jnp.float32)  23.2 us
    all_gather x1, waiting for transfers between devices, shards(): lax.all_gather(out_weight, 'dp', axis=2, tiled=True)  22.3 us
    ppermute x2, waiting for transfers between devices, from_partner(): lax.ppermute(shard, axis, [(i, i ^ 1 << distance) for i in range(lax.axis...  17.4 us
    dot_general x16, matrix products, attend(): jnp.einsum('hqk,khd->qhd', soft_weights.astype(jnp.float32), values)  13.7 us
  transfers between devices with their start and end apart: 12, of which 8 were waited for; matrix products, arithmetic and copies ran while one was open for 13% of the time, Pallas kernels for 0%

commit v1 on v0

v1 whole, which is shorter than its diff:
```python
import jax
import jax.numpy as jnp
from jax import lax
from jax.experimental import pallas as pl
from jax.experimental.pallas import tpu as pltpu
from jax.sharding import PartitionSpec as P

MESH = pl.DeviceIdType.MESH
BF = jnp.bfloat16
F32 = jnp.float32
D = 512
SEQ = 128
PAIRS = 4
SHARD = 64
LAYERS = 128


def nn(a, b):
    return lax.dot_general(a, b, (((1,), (0,)), ((), ())), preferred_element_type=F32)


def nt(a, b):
    return lax.dot_general(a, b, (((1,), (1,)), ((), ())), preferred_element_type=F32)


def tn(a, b):
    return lax.dot_general(a, b, (((0,), (0,)), ((), ())), preferred_element_type=F32)


def normalise(x):
    factor = lax.rsqrt(jnp.mean(x * x, axis=-1, keepdims=True) + 1e-05)
    return factor, (x * factor).astype(BF)


def split_heads(low, pair):
    zero = jnp.zeros_like(pair)
    return jnp.concatenate([jnp.where(low, pair, zero), jnp.where(low, zero, pair)], axis=0)


def side_by_side(both):
    return jnp.concatenate([both[:SEQ], both[SEQ:]], axis=1)


def masks():
    low = lax.broadcasted_iota(jnp.int32, (SEQ, SEQ), 1) < 64
    row = lax.broadcasted_iota(jnp.int32, (2 * SEQ, SEQ), 0)
    col = lax.broadcasted_iota(jnp.int32, (2 * SEQ, SEQ), 1)
    return low, col <= lax.rem(row, SEQ)


def attention(low, causal, queries, keys):
    scores = nt(queries, keys) * 0.125
    raised = jnp.where(causal, jnp.exp(scores), 0.0)
    return raised * (1.0 / jnp.sum(raised, axis=-1, keepdims=True))


def lanes(part, pair):
    return pl.ds(pl.multiple_of(part * D + pair * SEQ, SEQ), SEQ)


def forward(x_ref, wq_ref, wo_ref, qkv_ref, ctx_ref, out_ref):
    x = x_ref[...].astype(F32)
    _, normed = normalise(x)
    qkv_ref[...] = nn(normed, wq_ref[...]).astype(BF)
    low, causal = masks()

    def step(pair, carry):
        for g in range(2):
            rows = pl.ds(g * SEQ, SEQ)
            queries = split_heads(low, qkv_ref[rows, lanes(0, pair)])
            soft = attention(low, causal, queries, qkv_ref[rows, lanes(1, pair)]).astype(BF)
            values = split_heads(low, qkv_ref[rows, lanes(2, pair)])
            ctx_ref[rows, lanes(0, pair)] = nn(side_by_side(soft), values).astype(BF)
        return carry

    lax.fori_loop(0, PAIRS, step, 0)
    out_ref[...] = (x + nn(ctx_ref[...], wo_ref[...])).astype(BF)


def backward(
    first, x_ref, cot_ref, wq_ref, wo_ref, qkv_ref, ctx_ref, dctx_ref, dqkv_ref, accq_ref, acco_ref, out_ref
):
    x = x_ref[...].astype(F32)
    factor, normed = normalise(x)
    qkv_ref[...] = nn(normed, wq_ref[...]).astype(BF)
    cot = cot_ref[...]
    dctx_ref[...] = nt(cot, wo_ref[...]).astype(BF)
    low, causal = masks()

    def step(pair, carry):
        for g in range(2):
            rows = pl.ds(g * SEQ, SEQ)
            key_pair = qkv_ref[rows, lanes(1, pair)]
            value_pair = qkv_ref[rows, lanes(2, pair)]
            queries = split_heads(low, qkv_ref[rows, lanes(0, pair)])
            soft = attention(low, causal, queries, key_pair)
            soft_b = soft.astype(BF)
            ctx_ref[rows, lanes(0, pair)] = nn(side_by_side(soft_b), split_heads(low, value_pair)).astype(BF)
            dctx = split_heads(low, dctx_ref[rows, lanes(0, pair)])
            dsoft = nt(dctx, value_pair)
            dqkv_ref[rows, lanes(2, pair)] = tn(soft_b, dctx).astype(BF)
            dscore = soft * (dsoft - jnp.sum(soft * dsoft, axis=-1, keepdims=True))
            dscore = (dscore * 0.125).astype(BF)
            dqkv_ref[rows, lanes(0, pair)] = nn(side_by_side(dscore), split_heads(low, key_pair)).astype(BF)
            dqkv_ref[rows, lanes(1, pair)] = tn(dscore, queries).astype(BF)
        return carry

    lax.fori_loop(0, PAIRS, step, 0)
    dqkv = dqkv_ref[...]
    dnormed = nt(dqkv, wq_ref[...]).astype(BF).astype(F32)
    along = jnp.mean(dnormed * x, axis=-1, keepdims=True)
    dx = factor * dnormed - x * (factor * factor * factor * along)
    out_ref[...] = (cot.astype(F32) + dx).astype(BF)
    dwo = tn(ctx_ref[...], cot)
    dwq = tn(normed, dqkv)
    if first:
        acco_ref[...] = dwo
        accq_ref[...] = dwq
    else:
        acco_ref[...] += dwo
        accq_ref[...] += dwq


def kernel(
    wq_in, wo_in, act_in, cot_in, stash_in, arr_in, head_in,
    qg_out, og_out, na_out, nc_out,
    wq, wo, xs, cs, st, fo, bo, qkv, ctx, dctx, dqkv, accq, acco,
    gsq, gso, grq, gro, g2q, g2o, hgq, hgo, na, nc,
    s_w, r_w, s_f, r_f, s_x, r_x, s_c, r_c, s_st, r_st,
    s_fr, s_br, s_ff, r_ff, s_bf, r_bf, s_g1, r_g1, s_g2, r_g2, s_lo,
):
    s = lax.axis_index("section")
    d = lax.axis_index("dp")
    c = lax.rem(s, 2)
    plane = s // 2
    y = d // 4
    x = lax.rem(d, 4)
    lv = x // 2
    lc = lax.rem(x, 2)
    home = plane * 2 + lc
    layer = lv * 64 + home
    not_first = layer > 0
    not_last = layer < LAYERS - 1

    def worker(number, core, side):
        place = lax.rem(number, 64)
        return (place // 2 * 2 + core, side * 4 + number // 64 * 2 + lax.rem(place, 2))

    def other(device):
        return jnp.logical_or(device[0] != s, device[1] != d)

    sibling = (plane * 2 + 1 - c, d)
    kc = 1 - lax.rem(x, 2)
    up = lax.rem(layer + 1, LAYERS)
    down = lax.rem(layer + LAYERS - 1, LAYERS)
    upper = worker(up, c, y)
    lower = worker(down, c, y)
    group = [y * 4 + 2 * j + 1 - c for j in range(2)]
    shard = [yy * 4 + 2 * i + 1 - c for yy in range(2) for i in range(2)]
    sib_shard = [yy * 4 + 2 * i + c for yy in range(2) for i in range(2)]

    def rows_of(which):
        return pl.ds(pl.multiple_of(which * SHARD, SHARD), SHARD)

    def remote(src, dst, send, recv, device):
        return pltpu.make_async_remote_copy(
            src_ref=src, dst_ref=dst, send_sem=send, recv_sem=recv, device_id=device, device_id_type=MESH
        )

    weight_to = [worker(v * 64 + s, kc, yy) for v in range(2) for yy in range(2)]
    act_to = [worker(v * 64 + s, kc, y) for v in range(2)]
    stash_to = [worker(v * 64 + lax.rem(s + 32, 64), kc, y) for v in range(2)]
    stash_from = [(lax.rem(home + 32, 64), group[j]) for j in range(2)]
    grad_to = [(home, shard[k]) for k in range(4)]
    fwd_to = [(lax.rem(up, 64), group[j]) for j in range(2)]
    bwd_to = [(lax.rem(down, 64), group[j]) for j in range(2)]
    fwd_from = [worker(lax.rem(v * 64 + s + LAYERS - 1, LAYERS), kc, y) for v in range(2)]
    bwd_from = [worker(lax.rem(v * 64 + s + 1, LAYERS), kc, y) for v in range(2)]

    barrier = pltpu.get_barrier_semaphore()

    def greet(device):
        pl.semaphore_signal(barrier, inc=1, device_id=device, device_id_type=MESH)

    greet(sibling)
    for device in grad_to + weight_to + stash_from:
        greet(device)
    greet(lower)
    greet(upper)
    for device in fwd_from + bwd_from:
        pl.when(other(device))(lambda device=device: greet(device))
    greeted = 1 + 8 + 2 + 2
    for device in fwd_to + bwd_to:
        greeted = greeted + other(device).astype(jnp.int32)
    pl.semaphore_wait(barrier, greeted)

    slot = y * 2 + x // 2
    mine = rows_of(d)
    pending = []

    def send(*what):
        copy = remote(*what)
        copy.start()
        pending.append(copy)

    for n in range(4):
        v = n // 2
        send(wq_in.at[v, 0], wq.at[mine], s_w.at[n, 0], r_w.at[slot, 0], weight_to[n])
        send(wo_in.at[v, 0], wo.at[mine], s_w.at[n, 1], r_w.at[slot, 1], weight_to[n])
    j_here = x // 2
    seat = pl.ds(pl.multiple_of(j_here * SEQ, SEQ), SEQ)
    for v in range(2):
        send(act_in.at[v, 0, 0], xs.at[0, seat], s_x.at[v], r_x.at[0, j_here], act_to[v])
    for v in range(2):
        send(cot_in.at[v, 0, 0], cs.at[0, seat], s_c.at[v], r_c.at[0, j_here], act_to[v])

    def early(source, buffers, send_sem, recv_sem, device):
        return remote(source.at[0, 0], buffers.at[1, seat], send_sem, recv_sem.at[1, j_here], device)

    first_head = early(arr_in, xs, s_x.at[2], r_x, act_to[0])
    last_head = early(head_in, cs, s_c.at[2], r_c, act_to[1])
    pl.when(s == 0)(first_head.start)
    pl.when(s == 63)(last_head.start)
    for t in range(2):
        for v in range(2):
            send(
                stash_in.at[t, v, 0, 0], st.at[t, seat], s_st.at[t, v], r_st.at[t, j_here], stash_to[v]
            )

    forwards = []
    for k in range(4):
        rows = rows_of(shard[k])
        for part, ref in ((0, wq), (1, wo)):
            remote(ref.at[rows], ref.at[rows], s_f.at[k, part], r_w.at[k, part], sibling).wait_recv()
            copy = remote(ref.at[rows], ref.at[rows], s_f.at[k, part], r_f.at[k, part], sibling)
            copy.start()
            forwards.append(copy)
    for k in range(4):
        rows = rows_of(sib_shard[k])
        for part, ref in ((0, wq), (1, wo)):
            remote(ref.at[rows], ref.at[rows], s_f.at[k, part], r_f.at[k, part], sibling).wait_recv()

    def half(j):
        return pl.ds(j * SEQ, SEQ)

    def arrive(buffers, recv_sem, t):
        for j in range(2):
            ref = buffers.at[t, half(j)]
            remote(ref, ref, s_lo, recv_sem.at[t, j], sibling).wait_recv()

    def relay(source, buffers, send_sem, recv_sem, device):
        return [
            remote(source.at[0, half(j)], buffers.at[1, half(j)], send_sem.at[j], recv_sem.at[1, j], device)
            for j in range(2)
        ]

    def finish(source, landing, send_sem, recv_sem, devices, number):
        round_ = number // 64
        for j in range(2):
            src = source.at[1, half(j)]
            dst = landing.at[round_]
            copy = remote(src, dst, send_sem.at[j], recv_sem.at[round_], devices[j])
            own = pltpu.make_async_copy(src, dst, recv_sem.at[round_])
            yield copy, own, other(devices[j])

    def start_all(copies, allowed):
        for copy, own, away in copies:
            pl.when(jnp.logical_and(allowed, away))(copy.start)
            pl.when(jnp.logical_and(allowed, jnp.logical_not(away)))(own.start)

    fwd_relay = relay(fo, xs, s_fr, r_x, upper)
    bwd_relay = relay(bo, cs, s_br, r_c, lower)
    fwd_final = list(finish(fo, na, s_ff, r_ff, fwd_to, up))
    bwd_final = list(finish(bo, nc, s_bf, r_bf, bwd_to, down))

    def both(copies, allowed, what):
        def act():
            for copy in copies:
                getattr(copy, what)()

        pl.when(allowed)(act)

    arrive(xs, r_x, 0)
    forward(xs.at[0], wq, wo, qkv, ctx, fo.at[0])
    both(fwd_relay, not_last, "start")
    arrive(xs, r_x, 1)
    forward(xs.at[1], wq, wo, qkv, ctx, fo.at[1])
    start_all(fwd_final, not_last)

    arrive(cs, r_c, 0)
    arrive(st, r_st, 0)
    backward(True, st.at[0], cs.at[0], wq, wo, qkv, ctx, dctx, dqkv, accq, acco, bo.at[0])
    both(bwd_relay, not_first, "start")
    arrive(cs, r_c, 1)
    arrive(st, r_st, 1)
    backward(False, st.at[1], cs.at[1], wq, wo, qkv, ctx, dctx, dqkv, accq, acco, bo.at[1])
    start_all(bwd_final, not_first)

    for k in range(4):
        rows = rows_of(sib_shard[k])
        gsq[k] = accq[rows, :].astype(BF)
        gso[k] = acco[rows, :].astype(BF)
        send(gsq.at[k], grq.at[k], s_g1.at[k, 0], r_g1.at[k, 0], sibling)
        send(gso.at[k], gro.at[k], s_g1.at[k, 1], r_g1.at[k, 1], sibling)
    for k in range(4):
        rows = rows_of(shard[k])
        remote(gsq.at[k], grq.at[k], s_g1.at[k, 0], r_g1.at[k, 0], sibling).wait_recv()
        remote(gso.at[k], gro.at[k], s_g1.at[k, 1], r_g1.at[k, 1], sibling).wait_recv()
        g2q[k] = (accq[rows, :] + grq[k].astype(F32)).astype(BF)
        g2o[k] = (acco[rows, :] + gro[k].astype(F32)).astype(BF)
        send(g2q.at[k], hgq.at[lv, y], s_g2.at[k, 0], r_g2.at[lv, y, 0], grad_to[k])
        send(g2o.at[k], hgo.at[lv, y], s_g2.at[k, 1], r_g2.at[lv, y, 1], grad_to[k])

    own_arrival = pltpu.make_async_copy(arr_in.at[1, 0], na.at[0], r_ff.at[0])
    own_head = pltpu.make_async_copy(head_in.at[1, 0], nc.at[1], r_bf.at[1])
    pl.when(s == 0)(own_arrival.start)
    pl.when(s == 63)(own_head.start)
    for v in range(2):
        pltpu.make_async_copy(arr_in.at[1, 0], na.at[v], r_ff.at[v]).wait()
        na_out[v, 0, 0] = na[v]
        pltpu.make_async_copy(head_in.at[1, 0], nc.at[v], r_bf.at[v]).wait()
        nc_out[v, 0, 0] = nc[v]
    for v in range(2):
        for yy in range(2):
            remote(g2q.at[0], hgq.at[v, yy], s_g2.at[0, 0], r_g2.at[v, yy, 0], sibling).wait_recv()
            remote(g2o.at[0], hgo.at[v, yy], s_g2.at[0, 1], r_g2.at[v, yy, 1], sibling).wait_recv()
        qg_out[v, 0] = hgq[v, 0].astype(F32) + hgq[v, 1].astype(F32)
        og_out[v, 0] = hgo[v, 0].astype(F32) + hgo[v, 1].astype(F32)

    for copy in pending + forwards:
        copy.wait_send()
    pl.when(s == 0)(first_head.wait_send)
    pl.when(s == 63)(last_head.wait_send)
    both(fwd_relay, not_last, "wait_send")
    both(bwd_relay, not_first, "wait_send")
    for copies, allowed in ((fwd_final, not_last), (bwd_final, not_first)):
        for copy, own, away in copies:
            pl.when(jnp.logical_and(allowed, away))(copy.wait_send)


def shards(qkv_weight, out_weight, activations, cotangents, mirrored_stash, arrivals, head_grads):
    dma = pltpu.SemaphoreType.DMA
    hbm = pl.BlockSpec(memory_space=pl.ANY)
    vmem = pl.BlockSpec(memory_space=pltpu.VMEM)
    return pl.pallas_call(
        kernel,
        out_shape=(
            jax.ShapeDtypeStruct((2, 1, SHARD, 3 * D), F32),
            jax.ShapeDtypeStruct((2, 1, SHARD, D), F32),
            jax.ShapeDtypeStruct((2, 1, 1, SEQ, D), BF),
            jax.ShapeDtypeStruct((2, 1, 1, SEQ, D), BF),
        ),
        in_specs=[hbm] * 7,
        out_specs=[vmem] * 4,
        scratch_shapes=[
            pltpu.VMEM((D, 3 * D), BF),
            pltpu.VMEM((D, D), BF),
            pltpu.VMEM((2, 2 * SEQ, D), BF),
            pltpu.VMEM((2, 2 * SEQ, D), BF),
            pltpu.VMEM((2, 2 * SEQ, D), BF),
            pltpu.VMEM((2, 2 * SEQ, D), BF),
            pltpu.VMEM((2, 2 * SEQ, D), BF),
            pltpu.VMEM((2 * SEQ, 3 * D), BF),
            pltpu.VMEM((2 * SEQ, D), BF),
            pltpu.VMEM((2 * SEQ, D), BF),
            pltpu.VMEM((2 * SEQ, 3 * D), BF),
            pltpu.VMEM((D, 3 * D), F32),
            pltpu.VMEM((D, D), F32),
            pltpu.VMEM((4, SHARD, 3 * D), BF),
            pltpu.VMEM((4, SHARD, D), BF),
            pltpu.VMEM((4, SHARD, 3 * D), BF),
            pltpu.VMEM((4, SHARD, D), BF),
            pltpu.VMEM((4, SHARD, 3 * D), BF),
            pltpu.VMEM((4, SHARD, D), BF),
            pltpu.VMEM((2, 2, SHARD, 3 * D), BF),
            pltpu.VMEM((2, 2, SHARD, D), BF),
            pltpu.VMEM((2, SEQ, D), BF),
            pltpu.VMEM((2, SEQ, D), BF),
            dma((4, 2)), dma((4, 2)),
            dma((4, 2)), dma((4, 2)),
            dma((3,)), dma((2, 2)),
            dma((3,)), dma((2, 2)),
            dma((2, 2)), dma((2, 2)),
            dma((2,)), dma((2,)),
            dma((2,)), dma((2,)),
            dma((2,)), dma((2,)),
            dma((4, 2)), dma((4, 2)),
            dma((4, 2)), dma((2, 2, 2)),
            dma,
        ],
        compiler_params=pltpu.CompilerParams(
            collective_id=0, has_side_effects=True, vmem_limit_bytes=48 * 1024 * 1024
        ),
        cost_estimate=pl.CostEstimate(flops=5_000_000_000, bytes_accessed=8_000_000, transcendentals=2_000_000),
        name="window",
    )(qkv_weight, out_weight, activations, cotangents, mirrored_stash, arrivals, head_grads)


def solution(mesh):
    return jax.shard_map(
        shards,
        mesh=mesh,
        in_specs=(
            P(None, "section", "dp", None),
            P(None, "section", "dp", None),
            P(None, "section", "dp", None, None),
            P(None, "section", "dp", None, None),
            P(None, None, "section", "dp", None, None),
            P(None, "dp", None, None),
            P(None, "dp", None, None),
        ),
        out_specs=(
            P(None, "section", "dp", None),
            P(None, "section", "dp", None),
            P(None, "section", "dp", None, None),
            P(None, "section", "dp", None, None),
        ),
        check_vma=False,
    )
```

time: 354 us -> 119 us (0.34)
  the two profiles are of different devices: /device:TPU:16 before, /device:TPU:455 now
where the time goes in v1:
time: 119 us
  Pallas kernels  108 us (91%)
  local copies, waits for them, and re-layouts  9.72 us (8%)
    pallas_call x1, Pallas kernels, shards(): pl.pallas_call(kernel, out_shape=(jax.ShapeDtypeStruct((2, 1, SHARD, 3 *...  108 us
    unnamed x18, local copies, waits for them, and re-layouts  9.72 us

profile of v1, /device:TPU:455, one launch (start us, length us, event | category | flops | bytes accessed | tf_op | source)
XLA Modules:
  0.0 118.8 jit_solution(17583084008988236767)
XLA Ops:
  0.6 0.0 copy-start
  0.6 1.0 copy-done
  1.7 0.0 copy-start.1
  1.7 1.0 copy-done.1
  2.7 0.0 copy-start.2
  2.7 0.9 copy-done.2
  3.6 0.0 copy-start.3
  3.6 0.9 copy-done.3
  4.6 0.0 copy-start.4
  4.6 0.9 copy-done.4
  5.5 0.0 copy-start.5
  5.5 0.9 copy-done.5
  6.5 0.0 copy-start.6
  6.5 0.9 copy-done.6
  7.4 108.4 %window.1 = (f32[2,1,64,1536]{3,2,1,0:T(8,128)S(1)}, f32[2,1,64,512]{3,2,1,0:T(8,128)S(1)}, bf16[2,1,1,128,512]{4,3,2,1,0:T(8,128)(2,1)S(1)}, bf16[2,1,1,128,512]{4,3,2,1,0:T(8,128)(2,1)S(1)}) custom-call(bf16[2,1,64,1536]{3,2,1,0:T(8,128)(2,1)S(1)} %copy-done.1, bf16[2,1,64,512]{3,2,1,0:T(8,128)(2,1)S(1)} %copy-done.6, ...), custom_call_target="tpu_custom_call" | custom-call | flops 5000000000 | bytes 8000000 | tf_op jit(solution)/shard_map/window/pallas_call | solution.py:345
  115.8 0.9 copy.15
  116.7 0.7 copy.16
  117.4 0.7 copy.17
  118.1 0.7 copy.18
Async XLA Ops:
  0.6 1.0 copy-start
  1.7 1.0 copy-start.1
  2.7 0.9 copy-start.2
  3.6 0.9 copy-start.3
  4.6 0.9 copy-start.4
  5.5 0.9 copy-start.5
  6.5 0.9 copy-start.6

commit v2 on v1

--- a/solution.py
+++ b/solution.py
@@ -77,14 +77,12 @@
     out_ref[...] = (x + nn(ctx_ref[...], wo_ref[...])).astype(BF)
 
 
-def backward(
-    first, x_ref, cot_ref, wq_ref, wo_ref, qkv_ref, ctx_ref, dctx_ref, dqkv_ref, accq_ref, acco_ref, out_ref
-):
-    x = x_ref[...].astype(F32)
-    factor, normed = normalise(x)
+def backward(x_ref, cot_ref, wait_cot, wq_ref, wo_ref, qkv_ref, ctx_ref, dctx_ref, dqkv_ref, nrm_ref):
+    _, normed = normalise(x_ref[...].astype(F32))
+    nrm_ref[...] = normed
     qkv_ref[...] = nn(normed, wq_ref[...]).astype(BF)
-    cot = cot_ref[...]
-    dctx_ref[...] = nt(cot, wo_ref[...]).astype(BF)
+    wait_cot()
+    dctx_ref[...] = nt(cot_ref[...], wo_ref[...]).astype(BF)
     low, causal = masks()
 
     def step(pair, carry):
@@ -106,28 +104,24 @@
         return carry
 
     lax.fori_loop(0, PAIRS, step, 0)
-    dqkv = dqkv_ref[...]
-    dnormed = nt(dqkv, wq_ref[...]).astype(BF).astype(F32)
+
+
+def input_cotangent(x_ref, cot_ref, wq_ref, dqkv_ref, out_ref):
+    x = x_ref[...].astype(F32)
+    factor, _ = normalise(x)
+    dnormed = nt(dqkv_ref[...], wq_ref[...]).astype(BF).astype(F32)
     along = jnp.mean(dnormed * x, axis=-1, keepdims=True)
     dx = factor * dnormed - x * (factor * factor * factor * along)
-    out_ref[...] = (cot.astype(F32) + dx).astype(BF)
-    dwo = tn(ctx_ref[...], cot)
-    dwq = tn(normed, dqkv)
-    if first:
-        acco_ref[...] = dwo
-        accq_ref[...] = dwq
-    else:
-        acco_ref[...] += dwo
-        accq_ref[...] += dwq
+    out_ref[...] = (cot_ref[...].astype(F32) + dx).astype(BF)
 
 
 def kernel(
     wq_in, wo_in, act_in, cot_in, stash_in, arr_in, head_in,
-    qg_out, og_out, na_out, nc_out,
-    wq, wo, xs, cs, st, fo, bo, qkv, ctx, dctx, dqkv, accq, acco,
-    gsq, gso, grq, gro, g2q, g2o, hgq, hgo, na, nc,
+    hgq, hgo, na, nc,
+    wq, wo, xs, cs, st, fo, bo, qkv, ctx, dctx, dqkv, nrm, accq, acco,
+    gsq, gso, grq, gro, g2q, g2o,
     s_w, r_w, s_f, r_f, s_x, r_x, s_c, r_c, s_st, r_st,
-    s_fr, s_br, s_ff, r_ff, s_bf, r_bf, s_g1, r_g1, s_g2, r_g2, s_lo,
+    s_fr, s_br, s_ff, r_ff, s_bf, r_bf, s_g1, r_g1, s_g2, r_g2, s_lo, ans_relay, ans_final,
 ):
     s = lax.axis_index("section")
     d = lax.axis_index("dp")
@@ -136,7 +130,7 @@
     y = d // 4
     x = lax.rem(d, 4)
     lv = x // 2
-    lc = lax.rem(x, 2)
+    lc = lax.rem(x + y, 2)
     home = plane * 2 + lc
     layer = lv * 64 + home
     not_first = layer > 0
@@ -144,20 +138,20 @@
 
     def worker(number, core, side):
         place = lax.rem(number, 64)
-        return (place // 2 * 2 + core, side * 4 + number // 64 * 2 + lax.rem(place, 2))
+        return (place // 2 * 2 + core, side * 4 + number // 64 * 2 + lax.rem(place + side, 2))
 
     def other(device):
         return jnp.logical_or(device[0] != s, device[1] != d)
 
     sibling = (plane * 2 + 1 - c, d)
-    kc = 1 - lax.rem(x, 2)
+    kc = 1 - lax.rem(x + y, 2)
     up = lax.rem(layer + 1, LAYERS)
     down = lax.rem(layer + LAYERS - 1, LAYERS)
     upper = worker(up, c, y)
     lower = worker(down, c, y)
-    group = [y * 4 + 2 * j + 1 - c for j in range(2)]
-    shard = [yy * 4 + 2 * i + 1 - c for yy in range(2) for i in range(2)]
-    sib_shard = [yy * 4 + 2 * i + c for yy in range(2) for i in range(2)]
+    group = [y * 4 + 2 * j + lax.rem(1 - c + y, 2) for j in range(2)]
+    shard = [yy * 4 + 2 * i + lax.rem(1 - c + yy, 2) for yy in range(2) for i in range(2)]
+    sib_shard = [yy * 4 + 2 * i + lax.rem(c + yy, 2) for yy in range(2) for i in range(2)]
 
     def rows_of(which):
         return pl.ds(pl.multiple_of(which * SHARD, SHARD), SHARD)
@@ -186,13 +180,18 @@
     for device in grad_to + weight_to + stash_from:
         greet(device)
     greet(lower)
-    greet(upper)
-    for device in fwd_from + bwd_from:
-        pl.when(other(device))(lambda device=device: greet(device))
-    greeted = 1 + 8 + 2 + 2
-    for device in fwd_to + bwd_to:
-        greeted = greeted + other(device).astype(jnp.int32)
+    greeted = 1 + 8 + 2 + 1
+    for ours, theirs in zip(fwd_from + bwd_to, fwd_to + bwd_from):
+        pl.when(other(ours))(lambda device=ours: greet(device))
+        greeted = greeted + other(theirs).astype(jnp.int32)
     pl.semaphore_wait(barrier, greeted)
+
+    def answer(sem, device):
+        pl.semaphore_signal(sem, inc=1, device_id=device, device_id_type=MESH)
+
+    answer(ans_relay, upper)
+    for device in bwd_from:
+        pl.when(other(device))(lambda device=device: answer(ans_final, device))
 
     slot = y * 2 + x // 2
     mine = rows_of(d)
@@ -280,21 +279,29 @@
 
         pl.when(allowed)(act)
 
+    def arrive_cot(t):
+        return lambda: arrive(cs, r_c, t)
+
+    work = (wq, wo, qkv, ctx, dctx, dqkv, nrm)
+
     arrive(xs, r_x, 0)
     forward(xs.at[0], wq, wo, qkv, ctx, fo.at[0])
     both(fwd_relay, not_last, "start")
+    arrive(st, r_st, 0)
+    backward(st.at[0], cs.at[0], arrive_cot(0), *work)
+    input_cotangent(st.at[0], cs.at[0], wq, dqkv, bo.at[0])
+    pl.semaphore_wait(ans_relay, 1)
+    both(bwd_relay, not_first, "start")
+    acco[...] = tn(ctx[...], cs[0])
+    accq[...] = tn(nrm[...], dqkv[...])
+
     arrive(xs, r_x, 1)
     forward(xs.at[1], wq, wo, qkv, ctx, fo.at[1])
     start_all(fwd_final, not_last)
-
-    arrive(cs, r_c, 0)
-    arrive(st, r_st, 0)
-    backward(True, st.at[0], cs.at[0], wq, wo, qkv, ctx, dctx, dqkv, accq, acco, bo.at[0])
-    both(bwd_relay, not_first, "start")
-    arrive(cs, r_c, 1)
     arrive(st, r_st, 1)
-    backward(False, st.at[1], cs.at[1], wq, wo, qkv, ctx, dctx, dqkv, accq, acco, bo.at[1])
-    start_all(bwd_final, not_first)
+    backward(st.at[1], cs.at[1], arrive_cot(1), *work)
+    acco[...] += tn(ctx[...], cs[1])
+    accq[...] += tn(nrm[...], dqkv[...])
 
     for k in range(4):
         rows = rows_of(sib_shard[k])
@@ -311,21 +318,21 @@
         send(g2q.at[k], hgq.at[lv, y], s_g2.at[k, 0], r_g2.at[lv, y, 0], grad_to[k])
         send(g2o.at[k], hgo.at[lv, y], s_g2.at[k, 1], r_g2.at[lv, y, 1], grad_to[k])
 
+    input_cotangent(st.at[1], cs.at[1], wq, dqkv, bo.at[1])
+    pl.semaphore_wait(ans_final, sum(other(device).astype(jnp.int32) for device in bwd_to))
+    start_all(bwd_final, not_first)
+
     own_arrival = pltpu.make_async_copy(arr_in.at[1, 0], na.at[0], r_ff.at[0])
     own_head = pltpu.make_async_copy(head_in.at[1, 0], nc.at[1], r_bf.at[1])
     pl.when(s == 0)(own_arrival.start)
     pl.when(s == 63)(own_head.start)
     for v in range(2):
         pltpu.make_async_copy(arr_in.at[1, 0], na.at[v], r_ff.at[v]).wait()
-        na_out[v, 0, 0] = na[v]
         pltpu.make_async_copy(head_in.at[1, 0], nc.at[v], r_bf.at[v]).wait()
-        nc_out[v, 0, 0] = nc[v]
     for v in range(2):
         for yy in range(2):
             remote(g2q.at[0], hgq.at[v, yy], s_g2.at[0, 0], r_g2.at[v, yy, 0], sibling).wait_recv()
             remote(g2o.at[0], hgo.at[v, yy], s_g2.at[0, 1], r_g2.at[v, yy, 1], sibling).wait_recv()
-        qg_out[v, 0] = hgq[v, 0].astype(F32) + hgq[v, 1].astype(F32)
-        og_out[v, 0] = hgo[v, 0].astype(F32) + hgo[v, 1].astype(F32)
 
     for copy in pending + forwards:
         copy.wait_send()
@@ -338,20 +345,28 @@
             pl.when(jnp.logical_and(allowed, away))(copy.wait_send)
 
 
+def hand_over(hgq, hgo, na, nc, qkv_grad, out_grad, new_act, new_cot):
+    for v in range(2):
+        qkv_grad[v, 0] = hgq[v, 0].astype(F32) + hgq[v, 1].astype(F32)
+        out_grad[v, 0] = hgo[v, 0].astype(F32) + hgo[v, 1].astype(F32)
+        new_act[v, 0, 0] = na[v]
+        new_cot[v, 0, 0] = nc[v]
+
+
 def shards(qkv_weight, out_weight, activations, cotangents, mirrored_stash, arrivals, head_grads):
     dma = pltpu.SemaphoreType.DMA
     hbm = pl.BlockSpec(memory_space=pl.ANY)
     vmem = pl.BlockSpec(memory_space=pltpu.VMEM)
-    return pl.pallas_call(
+    results = pl.pallas_call(
         kernel,
         out_shape=(
-            jax.ShapeDtypeStruct((2, 1, SHARD, 3 * D), F32),
-            jax.ShapeDtypeStruct((2, 1, SHARD, D), F32),
-            jax.ShapeDtypeStruct((2, 1, 1, SEQ, D), BF),
-            jax.ShapeDtypeStruct((2, 1, 1, SEQ, D), BF),
+            jax.ShapeDtypeStruct((2, 2, SHARD, 3 * D), BF),
+            jax.ShapeDtypeStruct((2, 2, SHARD, D), BF),
+            jax.ShapeDtypeStruct((2, SEQ, D), BF),
+            jax.ShapeDtypeStruct((2, SEQ, D), BF),
         ),
         in_specs=[hbm] * 7,
-        out_specs=[vmem] * 4,
+        out_specs=[hbm] * 4,
         scratch_shapes=[
             pltpu.VMEM((D, 3 * D), BF),
             pltpu.VMEM((D, D), BF),
@@ -364,6 +379,7 @@
             pltpu.VMEM((2 * SEQ, D), BF),
             pltpu.VMEM((2 * SEQ, D), BF),
             pltpu.VMEM((2 * SEQ, 3 * D), BF),
+            pltpu.VMEM((2 * SEQ, D), BF),
             pltpu.VMEM((D, 3 * D), F32),
             pltpu.VMEM((D, D), F32),
             pltpu.VMEM((4, SHARD, 3 * D), BF),
@@ -372,10 +388,6 @@
             pltpu.VMEM((4, SHARD, D), BF),
             pltpu.VMEM((4, SHARD, 3 * D), BF),
             pltpu.VMEM((4, SHARD, D), BF),
-            pltpu.VMEM((2, 2, SHARD, 3 * D), BF),
-            pltpu.VMEM((2, 2, SHARD, D), BF),
-            pltpu.VMEM((2, SEQ, D), BF),
-            pltpu.VMEM((2, SEQ, D), BF),
             dma((4, 2)), dma((4, 2)),
             dma((4, 2)), dma((4, 2)),
             dma((3,)), dma((2, 2)),
@@ -387,13 +399,27 @@
             dma((4, 2)), dma((4, 2)),
             dma((4, 2)), dma((2, 2, 2)),
             dma,
+            pltpu.SemaphoreType.REGULAR,
+            pltpu.SemaphoreType.REGULAR,
         ],
         compiler_params=pltpu.CompilerParams(
-            collective_id=0, has_side_effects=True, vmem_limit_bytes=48 * 1024 * 1024
+            collective_id=0, has_side_effects=True, vmem_limit_bytes=62 * 1024 * 1024
         ),
         cost_estimate=pl.CostEstimate(flops=5_000_000_000, bytes_accessed=8_000_000, transcendentals=2_000_000),
         name="window",
     )(qkv_weight, out_weight, activations, cotangents, mirrored_stash, arrivals, head_grads)
+    return pl.pallas_call(
+        hand_over,
+        out_shape=(
+            jax.ShapeDtypeStruct((2, 1, SHARD, 3 * D), F32),
+            jax.ShapeDtypeStruct((2, 1, SHARD, D), F32),
+            jax.ShapeDtypeStruct((2, 1, 1, SEQ, D), BF),
+            jax.ShapeDtypeStruct((2, 1, 1, SEQ, D), BF),
+        ),
+        in_specs=[vmem] * 4,
+        out_specs=[vmem] * 4,
+        name="hand_over",
+    )(*results)
 
 
 def solution(mesh):

time: 119 us -> 91.9 us (0.77)
  the two profiles are of different devices: /device:TPU:455 before, /device:TPU:15 now
where the time goes in v2:
time: 91.9 us; the launch traced here: 91.8 us
  Pallas kernels  91.1 us (99%)
    pallas_call x1, Pallas kernels, shards(): pl.pallas_call(kernel, out_shape=(jax.ShapeDtypeStruct((2, 2, SHARD, 3 *...  88.6 us
    pallas_call x1, Pallas kernels, shards(): pl.pallas_call(hand_over, out_shape=(jax.ShapeDtypeStruct((2, 1, SHARD, 3...  2.52 us

profile of v2, /device:TPU:15, one launch (start us, length us, event | category | flops | bytes accessed | tf_op | source)
XLA Modules:
  0.0 91.8 jit_solution(7217792459827179396)
XLA Ops:
  0.6 88.6 %window.1 = (bf16[2,2,64,1536]{3,2,1,0:T(8,128)(2,1)}, bf16[2,2,64,512]{3,2,1,0:T(8,128)(2,1)}, bf16[2,128,512]{2,1,0:T(8,128)(2,1)}, bf16[2,128,512]{2,1,0:T(8,128)(2,1)}) custom-call(bf16[2,1,64,1536]{3,2,1,0:T(8,128)(2,1)} %wq_in.1, bf16[2,1,64,512]{3,2,1,0:T(8,128)(2,1)} %wo_in.1, bf16[2,1,1,128,512]{4,3,2,1,0:T(8,128)(2,1)} %act_in.1, ...), custom_call_target="tpu_custom_call" | custom-call | flops 5000000000 | bytes 8000000 | tf_op jit(solution)/shard_map/window/pallas_call | solution.py:360
  89.2 2.5 %hand_over.1 = (f32[2,1,64,1536]{3,2,1,0:T(8,128)}, f32[2,1,64,512]{3,2,1,0:T(8,128)}, bf16[2,1,1,128,512]{4,3,2,1,0:T(8,128)(2,1)}, bf16[2,1,1,128,512]{4,3,2,1,0:T(8,128)(2,1)}) custom-call(bf16[2,2,64,1536]{3,2,1,0:T(8,128)(2,1)} %get-tuple-element.8.hgq, bf16[2,2,64,512]{3,2,1,0:T(8,128)(2,1)} %get-tuple-element.9.hgo, ...), custom_call_target="tpu_custom_call" | custom-call | tf_op jit(solution)/shard_map/hand_over/pallas_call | solution.py:411

commit v3 on v2

--- a/solution.py
+++ b/solution.py
@@ -130,28 +130,38 @@
     y = d // 4
     x = lax.rem(d, 4)
     lv = x // 2
-    lc = lax.rem(x + y, 2)
+    lc = lax.rem(x + y + plane, 2)
     home = plane * 2 + lc
     layer = lv * 64 + home
     not_first = layer > 0
     not_last = layer < LAYERS - 1
 
+    def column(number, side):
+        place = lax.rem(number, 64)
+        return lax.rem(place + place // 2 + side, 2)
+
     def worker(number, core, side):
         place = lax.rem(number, 64)
-        return (place // 2 * 2 + core, side * 4 + number // 64 * 2 + lax.rem(place + side, 2))
+        return (place // 2 * 2 + core, side * 4 + number // 64 * 2 + column(number, side))
+
+    def core_of(number):
+        return 1 - lax.rem(x + y + lax.rem(number, 64) // 2, 2)
+
+    def same_groups(number):
+        return lax.rem(c + plane + lax.rem(number, 64) // 2, 2)
 
     def other(device):
         return jnp.logical_or(device[0] != s, device[1] != d)
 
     sibling = (plane * 2 + 1 - c, d)
-    kc = 1 - lax.rem(x + y, 2)
+    kc = core_of(s)
     up = lax.rem(layer + 1, LAYERS)
     down = lax.rem(layer + LAYERS - 1, LAYERS)
-    upper = worker(up, c, y)
-    lower = worker(down, c, y)
-    group = [y * 4 + 2 * j + lax.rem(1 - c + y, 2) for j in range(2)]
-    shard = [yy * 4 + 2 * i + lax.rem(1 - c + yy, 2) for yy in range(2) for i in range(2)]
-    sib_shard = [yy * 4 + 2 * i + lax.rem(c + yy, 2) for yy in range(2) for i in range(2)]
+    upper = worker(up, same_groups(up), y)
+    lower = worker(down, same_groups(down), y)
+    group = [y * 4 + 2 * j + lax.rem(1 - c + plane + y, 2) for j in range(2)]
+    shard = [yy * 4 + 2 * i + lax.rem(1 - c + plane + yy, 2) for yy in range(2) for i in range(2)]
+    sib_shard = [yy * 4 + 2 * i + lax.rem(c + plane + yy, 2) for yy in range(2) for i in range(2)]
 
     def rows_of(which):
         return pl.ds(pl.multiple_of(which * SHARD, SHARD), SHARD)
@@ -168,8 +178,10 @@
     grad_to = [(home, shard[k]) for k in range(4)]
     fwd_to = [(lax.rem(up, 64), group[j]) for j in range(2)]
     bwd_to = [(lax.rem(down, 64), group[j]) for j in range(2)]
-    fwd_from = [worker(lax.rem(v * 64 + s + LAYERS - 1, LAYERS), kc, y) for v in range(2)]
-    bwd_from = [worker(lax.rem(v * 64 + s + 1, LAYERS), kc, y) for v in range(2)]
+    before = [lax.rem(v * 64 + s + LAYERS - 1, LAYERS) for v in range(2)]
+    after = [lax.rem(v * 64 + s + 1, LAYERS) for v in range(2)]
+    fwd_from = [worker(number, core_of(number), y) for number in before]
+    bwd_from = [worker(number, core_of(number), y) for number in after]
 
     barrier = pltpu.get_barrier_semaphore()
 
@@ -220,11 +232,11 @@
     last_head = early(head_in, cs, s_c.at[2], r_c, act_to[1])
     pl.when(s == 0)(first_head.start)
     pl.when(s == 63)(last_head.start)
-    for t in range(2):
-        for v in range(2):
-            send(
-                stash_in.at[t, v, 0, 0], st.at[t, seat], s_st.at[t, v], r_st.at[t, j_here], stash_to[v]
-            )
+    def send_stash(t, v):
+        send(stash_in.at[t, v, 0, 0], st.at[t, seat], s_st.at[t, v], r_st.at[t, j_here], stash_to[v])
+
+    send_stash(0, 0)
+    send_stash(0, 1)
 
     forwards = []
     for k in range(4):
@@ -287,11 +299,13 @@
     arrive(xs, r_x, 0)
     forward(xs.at[0], wq, wo, qkv, ctx, fo.at[0])
     both(fwd_relay, not_last, "start")
+    send_stash(1, 0)
     arrive(st, r_st, 0)
     backward(st.at[0], cs.at[0], arrive_cot(0), *work)
     input_cotangent(st.at[0], cs.at[0], wq, dqkv, bo.at[0])
     pl.semaphore_wait(ans_relay, 1)
     both(bwd_relay, not_first, "start")
+    send_stash(1, 1)
     acco[...] = tn(ctx[...], cs[0])
     accq[...] = tn(nrm[...], dqkv[...])
 

time: 91.9 us -> 85.7 us (0.933)
  the two profiles are of different devices: /device:TPU:15 before, /device:TPU:8 now
where the time goes in v3:
time: 85.7 us; the launch traced here: 85.6 us
  Pallas kernels  85 us (99%)
    pallas_call x1, Pallas kernels, shards(): pl.pallas_call(kernel, out_shape=(jax.ShapeDtypeStruct((2, 2, SHARD, 3 *...  82.4 us
    pallas_call x1, Pallas kernels, shards(): pl.pallas_call(hand_over, out_shape=(jax.ShapeDtypeStruct((2, 1, SHARD, 3...  2.52 us

profile of v3, /device:TPU:8, one launch (start us, length us, event | category | flops | bytes accessed | tf_op | source)
XLA Modules:
  0.0 85.6 jit_solution(9365157983176206585)
XLA Ops:
  0.6 82.4 %window.1 = (bf16[2,2,64,1536]{3,2,1,0:T(8,128)(2,1)}, bf16[2,2,64,512]{3,2,1,0:T(8,128)(2,1)}, bf16[2,128,512]{2,1,0:T(8,128)(2,1)}, bf16[2,128,512]{2,1,0:T(8,128)(2,1)}) custom-call(bf16[2,1,64,1536]{3,2,1,0:T(8,128)(2,1)} %wq_in.1, bf16[2,1,64,512]{3,2,1,0:T(8,128)(2,1)} %wo_in.1, bf16[2,1,1,128,512]{4,3,2,1,0:T(8,128)(2,1)} %act_in.1, ...), custom_call_target="tpu_custom_call" | custom-call | flops 5000000000 | bytes 8000000 | tf_op jit(solution)/shard_map/window/pallas_call | solution.py:374
  83.1 2.5 %hand_over.1 = (f32[2,1,64,1536]{3,2,1,0:T(8,128)}, f32[2,1,64,512]{3,2,1,0:T(8,128)}, bf16[2,1,1,128,512]{4,3,2,1,0:T(8,128)(2,1)}, bf16[2,1,1,128,512]{4,3,2,1,0:T(8,128)(2,1)}) custom-call(bf16[2,2,64,1536]{3,2,1,0:T(8,128)(2,1)} %get-tuple-element.8.hgq, bf16[2,2,64,512]{3,2,1,0:T(8,128)(2,1)} %get-tuple-element.9.hgo, ...), custom_call_target="tpu_custom_call" | custom-call | tf_op jit(solution)/shard_map/hand_over/pallas_call | solution.py:425

commit v4 on v3

--- a/solution.py
+++ b/solution.py
@@ -73,7 +73,7 @@
             ctx_ref[rows, lanes(0, pair)] = nn(side_by_side(soft), values).astype(BF)
         return carry
 
-    lax.fori_loop(0, PAIRS, step, 0)
+    lax.fori_loop(0, PAIRS, step, 0, unroll=True)
     out_ref[...] = (x + nn(ctx_ref[...], wo_ref[...])).astype(BF)
 
 
@@ -103,7 +103,7 @@
             dqkv_ref[rows, lanes(1, pair)] = tn(dscore, queries).astype(BF)
         return carry
 
-    lax.fori_loop(0, PAIRS, step, 0)
+    lax.fori_loop(0, PAIRS, step, 0, unroll=True)
 
 
 def input_cotangent(x_ref, cot_ref, wq_ref, dqkv_ref, out_ref):

time: 85.7 us -> 85.1 us (level)
  the two profiles are of different devices: /device:TPU:8 before, /device:TPU:15 now
where the time goes in v4:
time: 85.1 us; the launch traced here: 84.8 us
  Pallas kernels  84.2 us (99%)
    pallas_call x1, Pallas kernels, shards(): pl.pallas_call(kernel, out_shape=(jax.ShapeDtypeStruct((2, 2, SHARD, 3 *...  81.7 us
    pallas_call x1, Pallas kernels, shards(): pl.pallas_call(hand_over, out_shape=(jax.ShapeDtypeStruct((2, 1, SHARD, 3...  2.52 us

profile of v4, /device:TPU:15, one launch (start us, length us, event | category | flops | bytes accessed | tf_op | source)
XLA Modules:
  0.0 84.8 jit_solution(10433864554718250013)
XLA Ops:
  0.6 81.7 %window.1 = (bf16[2,2,64,1536]{3,2,1,0:T(8,128)(2,1)}, bf16[2,2,64,512]{3,2,1,0:T(8,128)(2,1)}, bf16[2,128,512]{2,1,0:T(8,128)(2,1)}, bf16[2,128,512]{2,1,0:T(8,128)(2,1)}) custom-call(bf16[2,1,64,1536]{3,2,1,0:T(8,128)(2,1)} %wq_in.1, bf16[2,1,64,512]{3,2,1,0:T(8,128)(2,1)} %wo_in.1, bf16[2,1,1,128,512]{4,3,2,1,0:T(8,128)(2,1)} %act_in.1, ...), custom_call_target="tpu_custom_call" | custom-call | flops 5000000000 | bytes 8000000 | tf_op jit(solution)/shard_map/window/pallas_call | solution.py:374
  82.3 2.5 %hand_over.1 = (f32[2,1,64,1536]{3,2,1,0:T(8,128)}, f32[2,1,64,512]{3,2,1,0:T(8,128)}, bf16[2,1,1,128,512]{4,3,2,1,0:T(8,128)(2,1)}, bf16[2,1,1,128,512]{4,3,2,1,0:T(8,128)(2,1)}) custom-call(bf16[2,2,64,1536]{3,2,1,0:T(8,128)(2,1)} %get-tuple-element.8.hgq, bf16[2,2,64,512]{3,2,1,0:T(8,128)(2,1)} %get-tuple-element.9.hgo, ...), custom_call_target="tpu_custom_call" | custom-call | tf_op jit(solution)/shard_map/hand_over/pallas_call | solution.py:425
